TPU v7x, 32 devices: a whole 2x2x4 slice. The times are simulated.
32 devices in a mesh: wide: 16 (over z, y, core), narrow: 2 (over x).
Axes of the slice: x: 2, y: 2, z: 4, core: 2. Of those that a mesh axis runs over, the one named last changes fastest.
Arguments:
- fine_cot: float32 [2, 32, 128, 128], P(None, 'wide', 'narrow'), may hold values from -6 to 6
- obstacle: int32 [2, 32, 128, 128], P(None, 'wide', 'narrow'), may hold values 0 or 1
- sigma: float32 [32, 128, 128], P('wide', 'narrow'), may hold values from 0.2 to 20
Outputs:
- fine_adjoint: float32 [2, 32, 128, 128], P(None, 'wide', 'narrow')
- coarse_adjoint: float32 [16, 2, 16, 64], P('wide', 'narrow')
All inputs are finite; a program needn't handle non-finite values. No bound on the sum of `obstacle` on one device may be relied on, other than what follows from the above.
Results may differ from a plain program's by a relative error of at most 0.00011.
Values sent between devices are 32-bit elements; how exact they have to be, the bound alone decides.
A program may use at most 64 MiB of HBM per device.

v0:
```python
import jax
import jax.numpy as jnp
from jax import lax
from jax.sharding import PartitionSpec as P

SWEEPS = 4
OMEGA = 0.8
COEF_X = 1.0
COEF_Y = 1.0
COEF_Z = 4.0
SHIFT = 0.02


def with_halo(cells, sides, width):
    for axis, dim in sides:
        count = lax.axis_size(axis)
        ends = count - 1
        head = lax.slice_in_dim(cells, 0, width, axis=dim)
        tail = lax.slice_in_dim(cells, cells.shape[dim] - width, cells.shape[dim], axis=dim)
        cells = jnp.concatenate(
            [
                lax.ppermute(tail, axis, [(i, (i + 1) % count) for i in range(ends)]),
                cells,
                lax.ppermute(head, axis, [((i + 1) % count, i) for i in range(ends)]),
            ],
            axis=dim,
        )
    return cells


def sine_table(rows, cols, count):
    product = (rows[:, None] + 1) * (cols[None, :] + 1) % (2 * (count + 1))
    angle = jnp.pi * product.astype(jnp.float32) / (count + 1)
    return jnp.sqrt(2.0 / (count + 1)) * jnp.sin(angle)


def eigen_values(index, count):
    return 2.0 - 2.0 * jnp.cos(jnp.pi * (index + 1).astype(jnp.float32) / (count + 1))


def plane_transform(field):
    count_z = field.shape[2]
    count_y = field.shape[3]
    index_y = jnp.arange(count_y, dtype=jnp.int32)
    index_z = jnp.arange(count_z, dtype=jnp.int32)
    high = lax.Precision.HIGHEST
    field = jnp.einsum(
        "xdzy,yv->xdzv", field, sine_table(index_y, index_y, count_y), precision=high
    )
    return jnp.einsum("xdzv,zw->xdwv", field, sine_table(index_z, index_z, count_z), precision=high)


def plane_denominator(count_z, count_y):
    index_y = jnp.arange(count_y, dtype=jnp.int32)
    index_z = jnp.arange(count_z, dtype=jnp.int32)
    return (
        COEF_Y * eigen_values(index_y, count_y)[None, :]
        + COEF_Z * eigen_values(index_z, count_z)[:, None]
        + SHIFT
    )


def body(fine_cot, obstacle, sigma):
    diag = 6.0 + sigma
    fluid = obstacle.astype(jnp.float32)
    grad = fine_cot
    for sweep in range(SWEEPS):
        weighted = OMEGA * fluid * grad / diag
        padded = with_halo(weighted, (("wide", 1), ("narrow", 2)), 1)
        beside = padded[:, 2:, 1:-1] + padded[:, :-2, 1:-1]
        beside = beside + padded[:, 1:-1, 2:] + padded[:, 1:-1, :-2]
        vertical = jnp.pad(weighted, ((0, 0), (0, 0), (0, 0), (1, 1)))
        beside = beside + vertical[..., 2:] + vertical[..., :-2]
        grad = grad - diag * weighted + beside
    dirs, cells_x, cells_y, cells_z = grad.shape
    coarse = grad.reshape(dirs, cells_x // 2, 2, cells_y // 2, 2, cells_z // 8, 8).sum(
        axis=(2, 4, 6)
    )
    coarse = jnp.transpose(coarse, (1, 0, 3, 2))
    regrouped = lax.all_to_all(coarse, "narrow", split_axis=1, concat_axis=3, tiled=True)
    spectrum = plane_transform(regrouped)
    slabs = spectrum.shape[0]
    total_x = lax.axis_size("wide") * slabs
    own_rows = lax.axis_index("wide") * slabs + jnp.arange(slabs, dtype=jnp.int32)
    plane = plane_denominator(spectrum.shape[2], spectrum.shape[3])
    high = lax.Precision.HIGHEST

    def accumulate(piece):
        columns = jnp.arange(piece.shape[0], dtype=jnp.int32)
        table = sine_table(own_rows, columns, total_x)
        return jnp.einsum("kx,xdwv->kdwv", table, piece, precision=high)

    modes = accumulate(lax.all_gather(spectrum, "wide", axis=0, tiled=True))
    denom = COEF_X * eigen_values(own_rows, total_x)[:, None, None, None] + plane[None, None]
    back = plane_transform(modes / denom)
    coarse_adjoint = accumulate(lax.all_gather(back, "wide", axis=0, tiled=True))
    return (grad, coarse_adjoint)


def solution(mesh):
    placed = (
        P(None, "wide", "narrow", None),
        P(None, "wide", "narrow", None),
        P("wide", "narrow", None),
    )
    return jax.shard_map(
        body,
        mesh=mesh,
        in_specs=placed,
        out_specs=(P(None, "wide", "narrow", None), P("wide", "narrow", None, None)),
        check_vma=False,
    )
```

profile of v0, /device:TPU:0, one launch (start us, length us, event | category | flops | bytes accessed | tf_op | source)
XLA Modules:
  0.0 119.1 jit_solution(6856023964625204232)
XLA Ops:
  0.6 0.9 broadcast_add_fusion
  1.6 0.9 multiply_divide_fusion.3
  2.5 1.3 %collective-permute-start = (f32[2,1,64,128]{3,2,1,0:T(8,128)S(1)}, f32[2,1,64,128]{3,2,1,0:T(8,128)S(1)}, u32[]{:S(2)}, u32[]{:S(2)}) collective-permute-start(f32[2,1,64,128]{3,2,1,0:T(8,128)S(1)} %get-tuple-element.25), channel_id=1, source_target_pairs={{2,0},{4,2},{6,4},{8,6},{10,8},{12,10},{14,12},{16,14},{18,16},{20... | collective-permute-start | bytes 196616 | tf_op jit(solution)/shard_map/ppermute | solution.py:24
  3.8 3.2 %collective-permute-start.1 = (f32[2,1,64,128]{3,2,1,0:T(8,128)S(1)}, f32[2,1,64,128]{3,2,1,0:T(8,128)S(1)}, u32[]{:S(2)}, u32[]{:S(2)}) collective-permute-start(f32[2,1,64,128]{3,2,1,0:T(8,128)S(1)} %get-tuple-element.24), channel_id=1, source_target_pairs={{0,2},{2,4},{4,6},{6,8},{8,10},{10,12},{12,14},{14,16},{16,18},{18... | collective-permute-start | bytes 196616 | tf_op jit(solution)/shard_map/ppermute | solution.py:22
  7.0 0.9 collective-permute-done.1
  7.9 1.3 %collective-permute-start.2 = (f32[2,4,1,128]{3,2,1,0:T(1,128)S(1)}, f32[2,4,1,128]{3,2,1,0:T(1,128)S(1)}, u32[]{:S(2)}, u32[]{:S(2)}) collective-permute-start(f32[2,4,1,128]{3,2,1,0:T(1,128)S(1)} %get-tuple-element.16), channel_id=1, source_target_pairs={{1,0},{3,2},{5,4},{7,6},{9,8},{11,10},{13,12},{15,14},{17,16},{19,... | collective-permute-start | bytes 12296 | tf_op jit(solution)/shard_map/ppermute | solution.py:24
  9.2 4.8 %collective-permute-start.3 = (f32[2,4,1,128]{3,2,1,0:T(1,128)S(1)}, f32[2,4,1,128]{3,2,1,0:T(1,128)S(1)}, u32[]{:S(2)}, u32[]{:S(2)}) collective-permute-start(f32[2,4,1,128]{3,2,1,0:T(1,128)S(1)} %get-tuple-element.17), channel_id=1, source_target_pairs={{0,1},{2,3},{4,5},{6,7},{8,9},{10,11},{12,13},{14,15},{16,17},{18,... | collective-permute-start | bytes 12296 | tf_op jit(solution)/shard_map/ppermute | solution.py:22
  14.0 1.3 %collective-permute-done.3 = f32[2,4,1,128]{3,2,1,0:T(1,128)S(1)} collective-permute-done((f32[2,4,1,128]{3,2,1,0:T(1,128)S(1)}, f32[2,4,1,128]{3,2,1,0:T(1,128)S(1)}, u32[]{:S(2)}, u32[]{:S(2)}) %collective-permute-start.3) | collective-permute-done | bytes 4128 | tf_op jit(solution)/shard_map/ppermute | solution.py:22
  15.5 1.3 %collective-permute-start.4 = (f32[2,1,64,128]{3,2,1,0:T(8,128)S(1)}, f32[2,1,64,128]{3,2,1,0:T(8,128)S(1)}, u32[]{:S(2)}, u32[]{:S(2)}) collective-permute-start(f32[2,1,64,128]{3,2,1,0:T(8,128)S(1)} %get-tuple-element.23), channel_id=1, source_target_pairs={{2,0},{4,2},{6,4},{8,6},{10,8},{12,10},{14,12},{16,14},{18,16},{20... | collective-permute-start | bytes 196616 | tf_op jit(solution)/shard_map/ppermute | solution.py:24
  16.8 4.1 %collective-permute-start.5 = (f32[2,1,64,128]{3,2,1,0:T(8,128)S(1)}, f32[2,1,64,128]{3,2,1,0:T(8,128)S(1)}, u32[]{:S(2)}, u32[]{:S(2)}) collective-permute-start(f32[2,1,64,128]{3,2,1,0:T(8,128)S(1)} %get-tuple-element.22), channel_id=1, source_target_pairs={{0,2},{2,4},{4,6},{6,8},{8,10},{10,12},{12,14},{14,16},{16,18},{18... | collective-permute-start | bytes 196616 | tf_op jit(solution)/shard_map/ppermute | solution.py:22
  21.0 0.9 collective-permute-done.5
  21.8 1.3 %collective-permute-start.6 = (f32[2,4,1,128]{3,2,1,0:T(1,128)S(1)}, f32[2,4,1,128]{3,2,1,0:T(1,128)S(1)}, u32[]{:S(2)}, u32[]{:S(2)}) collective-permute-start(f32[2,4,1,128]{3,2,1,0:T(1,128)S(1)} %get-tuple-element.14), channel_id=1, source_target_pairs={{1,0},{3,2},{5,4},{7,6},{9,8},{11,10},{13,12},{15,14},{17,16},{19,... | collective-permute-start | bytes 12296 | tf_op jit(solution)/shard_map/ppermute | solution.py:24
  23.1 4.5 %collective-permute-start.7 = (f32[2,4,1,128]{3,2,1,0:T(1,128)S(1)}, f32[2,4,1,128]{3,2,1,0:T(1,128)S(1)}, u32[]{:S(2)}, u32[]{:S(2)}) collective-permute-start(f32[2,4,1,128]{3,2,1,0:T(1,128)S(1)} %get-tuple-element.15), channel_id=1, source_target_pairs={{0,1},{2,3},{4,5},{6,7},{8,9},{10,11},{12,13},{14,15},{16,17},{18,... | collective-permute-start | bytes 12296 | tf_op jit(solution)/shard_map/ppermute | solution.py:22
  27.7 1.3 %collective-permute-done.7 = f32[2,4,1,128]{3,2,1,0:T(1,128)S(1)} collective-permute-done((f32[2,4,1,128]{3,2,1,0:T(1,128)S(1)}, f32[2,4,1,128]{3,2,1,0:T(1,128)S(1)}, u32[]{:S(2)}, u32[]{:S(2)}) %collective-permute-start.7) | collective-permute-done | bytes 4128 | tf_op jit(solution)/shard_map/ppermute | solution.py:22
  29.2 1.3 %collective-permute-start.8 = (f32[2,1,64,128]{3,2,1,0:T(8,128)S(1)}, f32[2,1,64,128]{3,2,1,0:T(8,128)S(1)}, u32[]{:S(2)}, u32[]{:S(2)}) collective-permute-start(f32[2,1,64,128]{3,2,1,0:T(8,128)S(1)} %get-tuple-element.21), channel_id=1, source_target_pairs={{2,0},{4,2},{6,4},{8,6},{10,8},{12,10},{14,12},{16,14},{18,16},{20... | collective-permute-start | bytes 196616 | tf_op jit(solution)/shard_map/ppermute | solution.py:24
  30.5 5.8 %collective-permute-start.9 = (f32[2,1,64,128]{3,2,1,0:T(8,128)S(1)}, f32[2,1,64,128]{3,2,1,0:T(8,128)S(1)}, u32[]{:S(2)}, u32[]{:S(2)}) collective-permute-start(f32[2,1,64,128]{3,2,1,0:T(8,128)S(1)} %get-tuple-element.20), channel_id=1, source_target_pairs={{0,2},{2,4},{4,6},{6,8},{8,10},{10,12},{12,14},{14,16},{16,18},{18... | collective-permute-start | bytes 196616 | tf_op jit(solution)/shard_map/ppermute | solution.py:22
  36.3 0.9 collective-permute-done.9
  37.2 1.3 %collective-permute-start.10 = (f32[2,4,1,128]{3,2,1,0:T(1,128)S(1)}, f32[2,4,1,128]{3,2,1,0:T(1,128)S(1)}, u32[]{:S(2)}, u32[]{:S(2)}) collective-permute-start(f32[2,4,1,128]{3,2,1,0:T(1,128)S(1)} %get-tuple-element.12), channel_id=1, source_target_pairs={{1,0},{3,2},{5,4},{7,6},{9,8},{11,10},{13,12},{15,14},{17,16},{19,... | collective-permute-start | bytes 12296 | tf_op jit(solution)/shard_map/ppermute | solution.py:24
  38.5 4.5 %collective-permute-start.11 = (f32[2,4,1,128]{3,2,1,0:T(1,128)S(1)}, f32[2,4,1,128]{3,2,1,0:T(1,128)S(1)}, u32[]{:S(2)}, u32[]{:S(2)}) collective-permute-start(f32[2,4,1,128]{3,2,1,0:T(1,128)S(1)} %get-tuple-element.13), channel_id=1, source_target_pairs={{0,1},{2,3},{4,5},{6,7},{8,9},{10,11},{12,13},{14,15},{16,17},{18,... | collective-permute-start | bytes 12296 | tf_op jit(solution)/shard_map/ppermute | solution.py:22
  43.0 1.3 %collective-permute-done.11 = f32[2,4,1,128]{3,2,1,0:T(1,128)S(1)} collective-permute-done((f32[2,4,1,128]{3,2,1,0:T(1,128)S(1)}, f32[2,4,1,128]{3,2,1,0:T(1,128)S(1)}, u32[]{:S(2)}, u32[]{:S(2)}) %collective-permute-start.11) | collective-permute-done | bytes 4128 | tf_op jit(solution)/shard_map/ppermute | solution.py:22
  44.5 1.3 %collective-permute-start.12 = (f32[2,1,64,128]{3,2,1,0:T(8,128)S(1)}, f32[2,1,64,128]{3,2,1,0:T(8,128)S(1)}, u32[]{:S(2)}, u32[]{:S(2)}) collective-permute-start(f32[2,1,64,128]{3,2,1,0:T(8,128)S(1)} %get-tuple-element.19), channel_id=1, source_target_pairs={{2,0},{4,2},{6,4},{8,6},{10,8},{12,10},{14,12},{16,14},{18,16},{20... | collective-permute-start | bytes 196616 | tf_op jit(solution)/shard_map/ppermute | solution.py:24
  45.8 6.0 %collective-permute-start.13 = (f32[2,1,64,128]{3,2,1,0:T(8,128)S(1)}, f32[2,1,64,128]{3,2,1,0:T(8,128)S(1)}, u32[]{:S(2)}, u32[]{:S(2)}) collective-permute-start(f32[2,1,64,128]{3,2,1,0:T(8,128)S(1)} %get-tuple-element.18), channel_id=1, source_target_pairs={{0,2},{2,4},{4,6},{6,8},{8,10},{10,12},{12,14},{14,16},{16,18},{18... | collective-permute-start | bytes 196616 | tf_op jit(solution)/shard_map/ppermute | solution.py:22
  51.9 0.9 collective-permute-done.13
  52.7 1.3 %collective-permute-start.14 = (f32[2,4,1,128]{3,2,1,0:T(1,128)S(1)}, f32[2,4,1,128]{3,2,1,0:T(1,128)S(1)}, u32[]{:S(2)}, u32[]{:S(2)}) collective-permute-start(f32[2,4,1,128]{3,2,1,0:T(1,128)S(1)} %get-tuple-element.10), channel_id=1, source_target_pairs={{1,0},{3,2},{5,4},{7,6},{9,8},{11,10},{13,12},{15,14},{17,16},{19,... | collective-permute-start | bytes 12296 | tf_op jit(solution)/shard_map/ppermute | solution.py:24
  54.0 4.5 %collective-permute-start.15 = (f32[2,4,1,128]{3,2,1,0:T(1,128)S(1)}, f32[2,4,1,128]{3,2,1,0:T(1,128)S(1)}, u32[]{:S(2)}, u32[]{:S(2)}) collective-permute-start(f32[2,4,1,128]{3,2,1,0:T(1,128)S(1)} %get-tuple-element.11), channel_id=1, source_target_pairs={{0,1},{2,3},{4,5},{6,7},{8,9},{10,11},{12,13},{14,15},{16,17},{18,... | collective-permute-start | bytes 12296 | tf_op jit(solution)/shard_map/ppermute | solution.py:22
  58.6 1.3 %collective-permute-done.15 = f32[2,4,1,128]{3,2,1,0:T(1,128)S(1)} collective-permute-done((f32[2,4,1,128]{3,2,1,0:T(1,128)S(1)}, f32[2,4,1,128]{3,2,1,0:T(1,128)S(1)}, u32[]{:S(2)}, u32[]{:S(2)}) %collective-permute-start.15) | collective-permute-done | bytes 4128 | tf_op jit(solution)/shard_map/ppermute | solution.py:22
  59.9 0.8 fusion.118
  62.2 3.5 %all-to-all-start = ((f32[2,1,512]{2,1,0:T(1,128)}), f32[2,1,512]{2,1,0:T(1,128)S(1)}, u32[]{:S(2)}, u32[]{:S(2)}) async-start(f32[2,1,512]{2,1,0:T(1,128)} %reshape.164), calls=%async_computation | async-start | bytes 8192 | tf_op jit(solution)/shard_map/all_to_all | solution.py:80
  65.9 3.7 %all-to-all-done = f32[2,1,512]{2,1,0:T(1,128)S(1)} async-done(((f32[2,1,512]{2,1,0:T(1,128)}), f32[2,1,512]{2,1,0:T(1,128)S(1)}, u32[]{:S(2)}, u32[]{:S(2)}) %all-to-all-start) | async-done | bytes 4128 | tf_op jit(solution)/shard_map/all_to_all | solution.py:80
  71.6 27.9 %all-gather = f32[256,64]{1,0:T(8,128)S(1)} all-gather(f32[16,64]{1,0:T(8,128)S(1)} %fusion.64), channel_id=2, replica_groups=mesh['wide'=16,'narrow'=2] {'wide'}, dimensions={0}, use_global_device_ids=true | all-gather | bytes 69632 | tf_op jit(solution)/shard_map/all_gather | solution.py:93
  100.4 17.8 %all-gather.1 = f32[256,64]{1,0:T(8,128)S(1)} all-gather(f32[16,64]{1,0:T(8,128)S(1)} %fusion.62), channel_id=3, replica_groups=mesh['wide'=16,'narrow'=2] {'wide'}, dimensions={0}, use_global_device_ids=true | all-gather | bytes 69632 | tf_op jit(solution)/shard_map/all_gather | solution.py:96
  118.2 0.9 fusion.24
  (42 shorter events, 5.2 us)
Async XLA Ops:
  0.6 0.9 copy-start
  2.5 4.5 %collective-permute-start = (f32[2,1,64,128]{3,2,1,0:T(8,128)S(1)}, f32[2,1,64,128]{3,2,1,0:T(8,128)S(1)}, u32[]{:S(2)}, u32[]{:S(2)}) collective-permute-start(f32[2,1,64,128]{3,2,1,0:T(8,128)S(1)} %get-tuple-element.25), channel_id=1, source_target_pairs={{2,0},{4,2},{6,4},{8,6},{10,8},{12,10},{14,12},{16,14},{18,16},{20... | collective-permute-start | bytes 196616 | tf_op jit(solution)/shard_map/ppermute | solution.py:24
  3.8 11.5 %copy-start.1 = (f32[2,2,64,128]{3,2,1,0:T(8,128)S(1)}, f32[2,2,64,128]{3,2,1,0:T(8,128)}, u32[]{:S(2)}) copy-start(f32[2,2,64,128]{3,2,1,0:T(8,128)} %param.3) | copy-start | bytes 393220
  3.8 4.1 %collective-permute-start.1 = (f32[2,1,64,128]{3,2,1,0:T(8,128)S(1)}, f32[2,1,64,128]{3,2,1,0:T(8,128)S(1)}, u32[]{:S(2)}, u32[]{:S(2)}) collective-permute-start(f32[2,1,64,128]{3,2,1,0:T(8,128)S(1)} %get-tuple-element.24), channel_id=1, source_target_pairs={{0,2},{2,4},{4,6},{6,8},{8,10},{10,12},{12,14},{14,16},{16,18},{18... | collective-permute-start | bytes 196616 | tf_op jit(solution)/shard_map/ppermute | solution.py:22
  7.9 6.1 %collective-permute-start.2 = (f32[2,4,1,128]{3,2,1,0:T(1,128)S(1)}, f32[2,4,1,128]{3,2,1,0:T(1,128)S(1)}, u32[]{:S(2)}, u32[]{:S(2)}) collective-permute-start(f32[2,4,1,128]{3,2,1,0:T(1,128)S(1)} %get-tuple-element.16), channel_id=1, source_target_pairs={{1,0},{3,2},{5,4},{7,6},{9,8},{11,10},{13,12},{15,14},{17,16},{19,... | collective-permute-start | bytes 12296 | tf_op jit(solution)/shard_map/ppermute | solution.py:24
  9.2 6.2 %collective-permute-start.3 = (f32[2,4,1,128]{3,2,1,0:T(1,128)S(1)}, f32[2,4,1,128]{3,2,1,0:T(1,128)S(1)}, u32[]{:S(2)}, u32[]{:S(2)}) collective-permute-start(f32[2,4,1,128]{3,2,1,0:T(1,128)S(1)} %get-tuple-element.17), channel_id=1, source_target_pairs={{0,1},{2,3},{4,5},{6,7},{8,9},{10,11},{12,13},{14,15},{16,17},{18,... | collective-permute-start | bytes 12296 | tf_op jit(solution)/shard_map/ppermute | solution.py:22
  15.5 5.4 %collective-permute-start.4 = (f32[2,1,64,128]{3,2,1,0:T(8,128)S(1)}, f32[2,1,64,128]{3,2,1,0:T(8,128)S(1)}, u32[]{:S(2)}, u32[]{:S(2)}) collective-permute-start(f32[2,1,64,128]{3,2,1,0:T(8,128)S(1)} %get-tuple-element.23), channel_id=1, source_target_pairs={{2,0},{4,2},{6,4},{8,6},{10,8},{12,10},{14,12},{16,14},{18,16},{20... | collective-permute-start | bytes 196616 | tf_op jit(solution)/shard_map/ppermute | solution.py:24
  16.8 5.0 %collective-permute-start.5 = (f32[2,1,64,128]{3,2,1,0:T(8,128)S(1)}, f32[2,1,64,128]{3,2,1,0:T(8,128)S(1)}, u32[]{:S(2)}, u32[]{:S(2)}) collective-permute-start(f32[2,1,64,128]{3,2,1,0:T(8,128)S(1)} %get-tuple-element.22), channel_id=1, source_target_pairs={{0,2},{2,4},{4,6},{6,8},{8,10},{10,12},{12,14},{14,16},{16,18},{18... | collective-permute-start | bytes 196616 | tf_op jit(solution)/shard_map/ppermute | solution.py:22
  21.8 5.8 %collective-permute-start.6 = (f32[2,4,1,128]{3,2,1,0:T(1,128)S(1)}, f32[2,4,1,128]{3,2,1,0:T(1,128)S(1)}, u32[]{:S(2)}, u32[]{:S(2)}) collective-permute-start(f32[2,4,1,128]{3,2,1,0:T(1,128)S(1)} %get-tuple-element.14), channel_id=1, source_target_pairs={{1,0},{3,2},{5,4},{7,6},{9,8},{11,10},{13,12},{15,14},{17,16},{19,... | collective-permute-start | bytes 12296 | tf_op jit(solution)/shard_map/ppermute | solution.py:24
  23.1 5.9 %collective-permute-start.7 = (f32[2,4,1,128]{3,2,1,0:T(1,128)S(1)}, f32[2,4,1,128]{3,2,1,0:T(1,128)S(1)}, u32[]{:S(2)}, u32[]{:S(2)}) collective-permute-start(f32[2,4,1,128]{3,2,1,0:T(1,128)S(1)} %get-tuple-element.15), channel_id=1, source_target_pairs={{0,1},{2,3},{4,5},{6,7},{8,9},{10,11},{12,13},{14,15},{16,17},{18,... | collective-permute-start | bytes 12296 | tf_op jit(solution)/shard_map/ppermute | solution.py:22
  29.2 7.1 %collective-permute-start.8 = (f32[2,1,64,128]{3,2,1,0:T(8,128)S(1)}, f32[2,1,64,128]{3,2,1,0:T(8,128)S(1)}, u32[]{:S(2)}, u32[]{:S(2)}) collective-permute-start(f32[2,1,64,128]{3,2,1,0:T(8,128)S(1)} %get-tuple-element.21), channel_id=1, source_target_pairs={{2,0},{4,2},{6,4},{8,6},{10,8},{12,10},{14,12},{16,14},{18,16},{20... | collective-permute-start | bytes 196616 | tf_op jit(solution)/shard_map/ppermute | solution.py:24
  30.5 6.7 %collective-permute-start.9 = (f32[2,1,64,128]{3,2,1,0:T(8,128)S(1)}, f32[2,1,64,128]{3,2,1,0:T(8,128)S(1)}, u32[]{:S(2)}, u32[]{:S(2)}) collective-permute-start(f32[2,1,64,128]{3,2,1,0:T(8,128)S(1)} %get-tuple-element.20), channel_id=1, source_target_pairs={{0,2},{2,4},{4,6},{6,8},{8,10},{10,12},{12,14},{14,16},{16,18},{18... | collective-permute-start | bytes 196616 | tf_op jit(solution)/shard_map/ppermute | solution.py:22
  37.2 5.9 %collective-permute-start.10 = (f32[2,4,1,128]{3,2,1,0:T(1,128)S(1)}, f32[2,4,1,128]{3,2,1,0:T(1,128)S(1)}, u32[]{:S(2)}, u32[]{:S(2)}) collective-permute-start(f32[2,4,1,128]{3,2,1,0:T(1,128)S(1)} %get-tuple-element.12), channel_id=1, source_target_pairs={{1,0},{3,2},{5,4},{7,6},{9,8},{11,10},{13,12},{15,14},{17,16},{19,... | collective-permute-start | bytes 12296 | tf_op jit(solution)/shard_map/ppermute | solution.py:24
  38.5 5.9 %collective-permute-start.11 = (f32[2,4,1,128]{3,2,1,0:T(1,128)S(1)}, f32[2,4,1,128]{3,2,1,0:T(1,128)S(1)}, u32[]{:S(2)}, u32[]{:S(2)}) collective-permute-start(f32[2,4,1,128]{3,2,1,0:T(1,128)S(1)} %get-tuple-element.13), channel_id=1, source_target_pairs={{0,1},{2,3},{4,5},{6,7},{8,9},{10,11},{12,13},{14,15},{16,17},{18,... | collective-permute-start | bytes 12296 | tf_op jit(solution)/shard_map/ppermute | solution.py:22
  44.5 7.4 %collective-permute-start.12 = (f32[2,1,64,128]{3,2,1,0:T(8,128)S(1)}, f32[2,1,64,128]{3,2,1,0:T(8,128)S(1)}, u32[]{:S(2)}, u32[]{:S(2)}) collective-permute-start(f32[2,1,64,128]{3,2,1,0:T(8,128)S(1)} %get-tuple-element.19), channel_id=1, source_target_pairs={{2,0},{4,2},{6,4},{8,6},{10,8},{12,10},{14,12},{16,14},{18,16},{20... | collective-permute-start | bytes 196616 | tf_op jit(solution)/shard_map/ppermute | solution.py:24
  45.8 6.9 %collective-permute-start.13 = (f32[2,1,64,128]{3,2,1,0:T(8,128)S(1)}, f32[2,1,64,128]{3,2,1,0:T(8,128)S(1)}, u32[]{:S(2)}, u32[]{:S(2)}) collective-permute-start(f32[2,1,64,128]{3,2,1,0:T(8,128)S(1)} %get-tuple-element.18), channel_id=1, source_target_pairs={{0,2},{2,4},{4,6},{6,8},{8,10},{10,12},{12,14},{14,16},{16,18},{18... | collective-permute-start | bytes 196616 | tf_op jit(solution)/shard_map/ppermute | solution.py:22
  52.7 5.9 %collective-permute-start.14 = (f32[2,4,1,128]{3,2,1,0:T(1,128)S(1)}, f32[2,4,1,128]{3,2,1,0:T(1,128)S(1)}, u32[]{:S(2)}, u32[]{:S(2)}) collective-permute-start(f32[2,4,1,128]{3,2,1,0:T(1,128)S(1)} %get-tuple-element.10), channel_id=1, source_target_pairs={{1,0},{3,2},{5,4},{7,6},{9,8},{11,10},{13,12},{15,14},{17,16},{19,... | collective-permute-start | bytes 12296 | tf_op jit(solution)/shard_map/ppermute | solution.py:24
  54.0 5.9 %collective-permute-start.15 = (f32[2,4,1,128]{3,2,1,0:T(1,128)S(1)}, f32[2,4,1,128]{3,2,1,0:T(1,128)S(1)}, u32[]{:S(2)}, u32[]{:S(2)}) collective-permute-start(f32[2,4,1,128]{3,2,1,0:T(1,128)S(1)} %get-tuple-element.11), channel_id=1, source_target_pairs={{0,1},{2,3},{4,5},{6,7},{8,9},{10,11},{12,13},{14,15},{16,17},{18,... | collective-permute-start | bytes 12296 | tf_op jit(solution)/shard_map/ppermute | solution.py:22
  62.2 7.3 %all-to-all-start = ((f32[2,1,512]{2,1,0:T(1,128)}), f32[2,1,512]{2,1,0:T(1,128)S(1)}, u32[]{:S(2)}, u32[]{:S(2)}) async-start(f32[2,1,512]{2,1,0:T(1,128)} %reshape.164), calls=%async_computation | async-start | bytes 8192 | tf_op jit(solution)/shard_map/all_to_all | solution.py:80
where the time goes:
time: 120 us; the launch traced here: 119 us
  starting transfers between devices  51.4 us (43%)
  blocking collectives  45.7 us (38%)
  waiting for transfers between devices  12.3 us (10%)
  other arithmetic  4.09 us (3%)
  matrix products  2.44 us (2%)
  local copies, waits for them, and re-layouts  2.1 us (2%)
    ppermute x8, starting transfers between devices, with_halo(): lax.ppermute(tail, axis, [(i, (i + 1) % count) for i in range(ends)])  37.6 us
    all_gather x1, blocking collectives, body(): modes = accumulate(lax.all_gather(spectrum, 'wide', axis=0, tiled=True))  27.9 us
    all_gather x1, blocking collectives, body(): lax.all_gather(back, 'wide', axis=0, tiled=True)  17.8 us
    ppermute x8, starting transfers between devices, with_halo(): lax.ppermute(head, axis, [((i + 1) % count, i) for i in range(ends)])  10.3 us
    ppermute x8, waiting for transfers between devices, with_halo(): lax.ppermute(tail, axis, [(i, (i + 1) % count) for i in range(ends)])  8.62 us
    all_to_all x1, waiting for transfers between devices, body(): lax.all_to_all(coarse, 'narrow', split_axis=1, concat_axis=3, tiled=True)  3.66 us
    all_to_all x1, starting transfers between devices, body(): lax.all_to_all(coarse, 'narrow', split_axis=1, concat_axis=3, tiled=True)  3.55 us
  transfers between devices with their start and end apart: 17, of which 9 were waited for; matrix products, arithmetic and copies ran while one was open for 0% of the time, Pallas kernels for 0%

commit v1 on v0

--- a/solution.py
+++ b/solution.py
@@ -77,7 +77,10 @@
         axis=(2, 4, 6)
     )
     coarse = jnp.transpose(coarse, (1, 0, 3, 2))
-    regrouped = lax.all_to_all(coarse, "narrow", split_axis=1, concat_axis=3, tiled=True)
+    size = lax.axis_size("narrow")
+    blocks = jnp.stack(jnp.split(coarse, size, axis=1), axis=0)
+    blocks = lax.all_to_all(blocks, "narrow", split_axis=0, concat_axis=0)
+    regrouped = jnp.concatenate(blocks, axis=3)
     spectrum = plane_transform(regrouped)
     slabs = spectrum.shape[0]
     total_x = lax.axis_size("wide") * slabs

time: 120 us -> 120 us (level)
  no operation moved by 1% of the time
where the time goes in v1:
time: 120 us; the launch traced here: 119 us
  starting transfers between devices  51.4 us (43%)
  blocking collectives  45.7 us (38%)
  waiting for transfers between devices  12.3 us (10%)
  other arithmetic  4.1 us (3%)
  matrix products  2.44 us (2%)
  local copies, waits for them, and re-layouts  2.1 us (2%)
    ppermute x8, starting transfers between devices, with_halo(): lax.ppermute(tail, axis, [(i, (i + 1) % count) for i in range(ends)])  37.6 us
    all_gather x1, blocking collectives, body(): modes = accumulate(lax.all_gather(spectrum, 'wide', axis=0, tiled=True))  27.9 us
    all_gather x1, blocking collectives, body(): lax.all_gather(back, 'wide', axis=0, tiled=True)  17.8 us
    ppermute x8, starting transfers between devices, with_halo(): lax.ppermute(head, axis, [((i + 1) % count, i) for i in range(ends)])  10.3 us
    ppermute x8, waiting for transfers between devices, with_halo(): lax.ppermute(tail, axis, [(i, (i + 1) % count) for i in range(ends)])  8.62 us
    all_to_all x1, waiting for transfers between devices, body(): blocks = lax.all_to_all(blocks, 'narrow', split_axis=0, concat_axis=0)  3.66 us
    all_to_all x1, starting transfers between devices, body(): blocks = lax.all_to_all(blocks, 'narrow', split_axis=0, concat_axis=0)  3.55 us
  transfers between devices with their start and end apart: 17, of which 9 were waited for; matrix products, arithmetic and copies ran while one was open for 0% of the time, Pallas kernels for 0%

profile of v1, /device:TPU:0, one launch (start us, length us, event | category | flops | bytes accessed | tf_op | source)
XLA Modules:
  0.0 119.1 jit_solution(4796031338043887256)
XLA Ops:
  0.6 0.9 broadcast_add_fusion
  1.6 0.9 multiply_divide_fusion.3
  2.5 1.3 %collective-permute-start = (f32[2,1,64,128]{3,2,1,0:T(8,128)S(1)}, f32[2,1,64,128]{3,2,1,0:T(8,128)S(1)}, u32[]{:S(2)}, u32[]{:S(2)}) collective-permute-start(f32[2,1,64,128]{3,2,1,0:T(8,128)S(1)} %get-tuple-element.25), channel_id=1, source_target_pairs={{2,0},{4,2},{6,4},{8,6},{10,8},{12,10},{14,12},{16,14},{18,16},{20... | collective-permute-start | bytes 196616 | tf_op jit(solution)/shard_map/ppermute | solution.py:24
  3.8 3.2 %collective-permute-start.1 = (f32[2,1,64,128]{3,2,1,0:T(8,128)S(1)}, f32[2,1,64,128]{3,2,1,0:T(8,128)S(1)}, u32[]{:S(2)}, u32[]{:S(2)}) collective-permute-start(f32[2,1,64,128]{3,2,1,0:T(8,128)S(1)} %get-tuple-element.24), channel_id=1, source_target_pairs={{0,2},{2,4},{4,6},{6,8},{8,10},{10,12},{12,14},{14,16},{16,18},{18... | collective-permute-start | bytes 196616 | tf_op jit(solution)/shard_map/ppermute | solution.py:22
  7.0 0.9 collective-permute-done.1
  7.9 1.3 %collective-permute-start.2 = (f32[2,4,1,128]{3,2,1,0:T(1,128)S(1)}, f32[2,4,1,128]{3,2,1,0:T(1,128)S(1)}, u32[]{:S(2)}, u32[]{:S(2)}) collective-permute-start(f32[2,4,1,128]{3,2,1,0:T(1,128)S(1)} %get-tuple-element.16), channel_id=1, source_target_pairs={{1,0},{3,2},{5,4},{7,6},{9,8},{11,10},{13,12},{15,14},{17,16},{19,... | collective-permute-start | bytes 12296 | tf_op jit(solution)/shard_map/ppermute | solution.py:24
  9.2 4.8 %collective-permute-start.3 = (f32[2,4,1,128]{3,2,1,0:T(1,128)S(1)}, f32[2,4,1,128]{3,2,1,0:T(1,128)S(1)}, u32[]{:S(2)}, u32[]{:S(2)}) collective-permute-start(f32[2,4,1,128]{3,2,1,0:T(1,128)S(1)} %get-tuple-element.17), channel_id=1, source_target_pairs={{0,1},{2,3},{4,5},{6,7},{8,9},{10,11},{12,13},{14,15},{16,17},{18,... | collective-permute-start | bytes 12296 | tf_op jit(solution)/shard_map/ppermute | solution.py:22
  14.0 1.3 %collective-permute-done.3 = f32[2,4,1,128]{3,2,1,0:T(1,128)S(1)} collective-permute-done((f32[2,4,1,128]{3,2,1,0:T(1,128)S(1)}, f32[2,4,1,128]{3,2,1,0:T(1,128)S(1)}, u32[]{:S(2)}, u32[]{:S(2)}) %collective-permute-start.3) | collective-permute-done | bytes 4128 | tf_op jit(solution)/shard_map/ppermute | solution.py:22
  15.5 1.3 %collective-permute-start.4 = (f32[2,1,64,128]{3,2,1,0:T(8,128)S(1)}, f32[2,1,64,128]{3,2,1,0:T(8,128)S(1)}, u32[]{:S(2)}, u32[]{:S(2)}) collective-permute-start(f32[2,1,64,128]{3,2,1,0:T(8,128)S(1)} %get-tuple-element.23), channel_id=1, source_target_pairs={{2,0},{4,2},{6,4},{8,6},{10,8},{12,10},{14,12},{16,14},{18,16},{20... | collective-permute-start | bytes 196616 | tf_op jit(solution)/shard_map/ppermute | solution.py:24
  16.8 4.1 %collective-permute-start.5 = (f32[2,1,64,128]{3,2,1,0:T(8,128)S(1)}, f32[2,1,64,128]{3,2,1,0:T(8,128)S(1)}, u32[]{:S(2)}, u32[]{:S(2)}) collective-permute-start(f32[2,1,64,128]{3,2,1,0:T(8,128)S(1)} %get-tuple-element.22), channel_id=1, source_target_pairs={{0,2},{2,4},{4,6},{6,8},{8,10},{10,12},{12,14},{14,16},{16,18},{18... | collective-permute-start | bytes 196616 | tf_op jit(solution)/shard_map/ppermute | solution.py:22
  21.0 0.9 collective-permute-done.5
  21.8 1.3 %collective-permute-start.6 = (f32[2,4,1,128]{3,2,1,0:T(1,128)S(1)}, f32[2,4,1,128]{3,2,1,0:T(1,128)S(1)}, u32[]{:S(2)}, u32[]{:S(2)}) collective-permute-start(f32[2,4,1,128]{3,2,1,0:T(1,128)S(1)} %get-tuple-element.14), channel_id=1, source_target_pairs={{1,0},{3,2},{5,4},{7,6},{9,8},{11,10},{13,12},{15,14},{17,16},{19,... | collective-permute-start | bytes 12296 | tf_op jit(solution)/shard_map/ppermute | solution.py:24
  23.1 4.5 %collective-permute-start.7 = (f32[2,4,1,128]{3,2,1,0:T(1,128)S(1)}, f32[2,4,1,128]{3,2,1,0:T(1,128)S(1)}, u32[]{:S(2)}, u32[]{:S(2)}) collective-permute-start(f32[2,4,1,128]{3,2,1,0:T(1,128)S(1)} %get-tuple-element.15), channel_id=1, source_target_pairs={{0,1},{2,3},{4,5},{6,7},{8,9},{10,11},{12,13},{14,15},{16,17},{18,... | collective-permute-start | bytes 12296 | tf_op jit(solution)/shard_map/ppermute | solution.py:22
  27.7 1.3 %collective-permute-done.7 = f32[2,4,1,128]{3,2,1,0:T(1,128)S(1)} collective-permute-done((f32[2,4,1,128]{3,2,1,0:T(1,128)S(1)}, f32[2,4,1,128]{3,2,1,0:T(1,128)S(1)}, u32[]{:S(2)}, u32[]{:S(2)}) %collective-permute-start.7) | collective-permute-done | bytes 4128 | tf_op jit(solution)/shard_map/ppermute | solution.py:22
  29.2 1.3 %collective-permute-start.8 = (f32[2,1,64,128]{3,2,1,0:T(8,128)S(1)}, f32[2,1,64,128]{3,2,1,0:T(8,128)S(1)}, u32[]{:S(2)}, u32[]{:S(2)}) collective-permute-start(f32[2,1,64,128]{3,2,1,0:T(8,128)S(1)} %get-tuple-element.21), channel_id=1, source_target_pairs={{2,0},{4,2},{6,4},{8,6},{10,8},{12,10},{14,12},{16,14},{18,16},{20... | collective-permute-start | bytes 196616 | tf_op jit(solution)/shard_map/ppermute | solution.py:24
  30.5 5.8 %collective-permute-start.9 = (f32[2,1,64,128]{3,2,1,0:T(8,128)S(1)}, f32[2,1,64,128]{3,2,1,0:T(8,128)S(1)}, u32[]{:S(2)}, u32[]{:S(2)}) collective-permute-start(f32[2,1,64,128]{3,2,1,0:T(8,128)S(1)} %get-tuple-element.20), channel_id=1, source_target_pairs={{0,2},{2,4},{4,6},{6,8},{8,10},{10,12},{12,14},{14,16},{16,18},{18... | collective-permute-start | bytes 196616 | tf_op jit(solution)/shard_map/ppermute | solution.py:22
  36.3 0.9 collective-permute-done.9
  37.2 1.3 %collective-permute-start.10 = (f32[2,4,1,128]{3,2,1,0:T(1,128)S(1)}, f32[2,4,1,128]{3,2,1,0:T(1,128)S(1)}, u32[]{:S(2)}, u32[]{:S(2)}) collective-permute-start(f32[2,4,1,128]{3,2,1,0:T(1,128)S(1)} %get-tuple-element.12), channel_id=1, source_target_pairs={{1,0},{3,2},{5,4},{7,6},{9,8},{11,10},{13,12},{15,14},{17,16},{19,... | collective-permute-start | bytes 12296 | tf_op jit(solution)/shard_map/ppermute | solution.py:24
  38.5 4.5 %collective-permute-start.11 = (f32[2,4,1,128]{3,2,1,0:T(1,128)S(1)}, f32[2,4,1,128]{3,2,1,0:T(1,128)S(1)}, u32[]{:S(2)}, u32[]{:S(2)}) collective-permute-start(f32[2,4,1,128]{3,2,1,0:T(1,128)S(1)} %get-tuple-element.13), channel_id=1, source_target_pairs={{0,1},{2,3},{4,5},{6,7},{8,9},{10,11},{12,13},{14,15},{16,17},{18,... | collective-permute-start | bytes 12296 | tf_op jit(solution)/shard_map/ppermute | solution.py:22
  43.0 1.3 %collective-permute-done.11 = f32[2,4,1,128]{3,2,1,0:T(1,128)S(1)} collective-permute-done((f32[2,4,1,128]{3,2,1,0:T(1,128)S(1)}, f32[2,4,1,128]{3,2,1,0:T(1,128)S(1)}, u32[]{:S(2)}, u32[]{:S(2)}) %collective-permute-start.11) | collective-permute-done | bytes 4128 | tf_op jit(solution)/shard_map/ppermute | solution.py:22
  44.5 1.3 %collective-permute-start.12 = (f32[2,1,64,128]{3,2,1,0:T(8,128)S(1)}, f32[2,1,64,128]{3,2,1,0:T(8,128)S(1)}, u32[]{:S(2)}, u32[]{:S(2)}) collective-permute-start(f32[2,1,64,128]{3,2,1,0:T(8,128)S(1)} %get-tuple-element.19), channel_id=1, source_target_pairs={{2,0},{4,2},{6,4},{8,6},{10,8},{12,10},{14,12},{16,14},{18,16},{20... | collective-permute-start | bytes 196616 | tf_op jit(solution)/shard_map/ppermute | solution.py:24
  45.8 6.0 %collective-permute-start.13 = (f32[2,1,64,128]{3,2,1,0:T(8,128)S(1)}, f32[2,1,64,128]{3,2,1,0:T(8,128)S(1)}, u32[]{:S(2)}, u32[]{:S(2)}) collective-permute-start(f32[2,1,64,128]{3,2,1,0:T(8,128)S(1)} %get-tuple-element.18), channel_id=1, source_target_pairs={{0,2},{2,4},{4,6},{6,8},{8,10},{10,12},{12,14},{14,16},{16,18},{18... | collective-permute-start | bytes 196616 | tf_op jit(solution)/shard_map/ppermute | solution.py:22
  51.9 0.9 collective-permute-done.13
  52.7 1.3 %collective-permute-start.14 = (f32[2,4,1,128]{3,2,1,0:T(1,128)S(1)}, f32[2,4,1,128]{3,2,1,0:T(1,128)S(1)}, u32[]{:S(2)}, u32[]{:S(2)}) collective-permute-start(f32[2,4,1,128]{3,2,1,0:T(1,128)S(1)} %get-tuple-element.10), channel_id=1, source_target_pairs={{1,0},{3,2},{5,4},{7,6},{9,8},{11,10},{13,12},{15,14},{17,16},{19,... | collective-permute-start | bytes 12296 | tf_op jit(solution)/shard_map/ppermute | solution.py:24
  54.0 4.5 %collective-permute-start.15 = (f32[2,4,1,128]{3,2,1,0:T(1,128)S(1)}, f32[2,4,1,128]{3,2,1,0:T(1,128)S(1)}, u32[]{:S(2)}, u32[]{:S(2)}) collective-permute-start(f32[2,4,1,128]{3,2,1,0:T(1,128)S(1)} %get-tuple-element.11), channel_id=1, source_target_pairs={{0,1},{2,3},{4,5},{6,7},{8,9},{10,11},{12,13},{14,15},{16,17},{18,... | collective-permute-start | bytes 12296 | tf_op jit(solution)/shard_map/ppermute | solution.py:22
  58.6 1.3 %collective-permute-done.15 = f32[2,4,1,128]{3,2,1,0:T(1,128)S(1)} collective-permute-done((f32[2,4,1,128]{3,2,1,0:T(1,128)S(1)}, f32[2,4,1,128]{3,2,1,0:T(1,128)S(1)}, u32[]{:S(2)}, u32[]{:S(2)}) %collective-permute-start.15) | collective-permute-done | bytes 4128 | tf_op jit(solution)/shard_map/ppermute | solution.py:22
  59.9 0.8 fusion.118
  62.3 3.5 %all-to-all-start = ((f32[2,1,512]{2,1,0:T(1,128)}), f32[2,1,512]{2,1,0:T(1,128)S(1)}, u32[]{:S(2)}, u32[]{:S(2)}) async-start(f32[2,1,512]{2,1,0:T(1,128)} %reshape.169), calls=%async_computation | async-start | bytes 8192 | tf_op jit(solution)/shard_map/all_to_all | solution.py:82
  65.9 3.7 %all-to-all-done = f32[2,1,512]{2,1,0:T(1,128)S(1)} async-done(((f32[2,1,512]{2,1,0:T(1,128)}), f32[2,1,512]{2,1,0:T(1,128)S(1)}, u32[]{:S(2)}, u32[]{:S(2)}) %all-to-all-start) | async-done | bytes 4128 | tf_op jit(solution)/shard_map/all_to_all | solution.py:82
  71.6 27.9 %all-gather = f32[256,64]{1,0:T(8,128)S(1)} all-gather(f32[16,64]{1,0:T(8,128)S(1)} %fusion.64), channel_id=2, replica_groups=mesh['wide'=16,'narrow'=2] {'wide'}, dimensions={0}, use_global_device_ids=true | all-gather | bytes 69632 | tf_op jit(solution)/shard_map/all_gather | solution.py:96
  100.4 17.8 %all-gather.1 = f32[256,64]{1,0:T(8,128)S(1)} all-gather(f32[16,64]{1,0:T(8,128)S(1)} %fusion.62), channel_id=3, replica_groups=mesh['wide'=16,'narrow'=2] {'wide'}, dimensions={0}, use_global_device_ids=true | all-gather | bytes 69632 | tf_op jit(solution)/shard_map/all_gather | solution.py:99
  118.2 0.9 fusion.24
  (43 shorter events, 5.2 us)
Async XLA Ops:
  0.6 0.9 copy-start
  2.5 4.5 %collective-permute-start = (f32[2,1,64,128]{3,2,1,0:T(8,128)S(1)}, f32[2,1,64,128]{3,2,1,0:T(8,128)S(1)}, u32[]{:S(2)}, u32[]{:S(2)}) collective-permute-start(f32[2,1,64,128]{3,2,1,0:T(8,128)S(1)} %get-tuple-element.25), channel_id=1, source_target_pairs={{2,0},{4,2},{6,4},{8,6},{10,8},{12,10},{14,12},{16,14},{18,16},{20... | collective-permute-start | bytes 196616 | tf_op jit(solution)/shard_map/ppermute | solution.py:24
  3.8 11.5 %copy-start.1 = (f32[2,2,64,128]{3,2,1,0:T(8,128)S(1)}, f32[2,2,64,128]{3,2,1,0:T(8,128)}, u32[]{:S(2)}) copy-start(f32[2,2,64,128]{3,2,1,0:T(8,128)} %param.3) | copy-start | bytes 393220
  3.8 4.1 %collective-permute-start.1 = (f32[2,1,64,128]{3,2,1,0:T(8,128)S(1)}, f32[2,1,64,128]{3,2,1,0:T(8,128)S(1)}, u32[]{:S(2)}, u32[]{:S(2)}) collective-permute-start(f32[2,1,64,128]{3,2,1,0:T(8,128)S(1)} %get-tuple-element.24), channel_id=1, source_target_pairs={{0,2},{2,4},{4,6},{6,8},{8,10},{10,12},{12,14},{14,16},{16,18},{18... | collective-permute-start | bytes 196616 | tf_op jit(solution)/shard_map/ppermute | solution.py:22
  7.9 6.1 %collective-permute-start.2 = (f32[2,4,1,128]{3,2,1,0:T(1,128)S(1)}, f32[2,4,1,128]{3,2,1,0:T(1,128)S(1)}, u32[]{:S(2)}, u32[]{:S(2)}) collective-permute-start(f32[2,4,1,128]{3,2,1,0:T(1,128)S(1)} %get-tuple-element.16), channel_id=1, source_target_pairs={{1,0},{3,2},{5,4},{7,6},{9,8},{11,10},{13,12},{15,14},{17,16},{19,... | collective-permute-start | bytes 12296 | tf_op jit(solution)/shard_map/ppermute | solution.py:24
  9.2 6.2 %collective-permute-start.3 = (f32[2,4,1,128]{3,2,1,0:T(1,128)S(1)}, f32[2,4,1,128]{3,2,1,0:T(1,128)S(1)}, u32[]{:S(2)}, u32[]{:S(2)}) collective-permute-start(f32[2,4,1,128]{3,2,1,0:T(1,128)S(1)} %get-tuple-element.17), channel_id=1, source_target_pairs={{0,1},{2,3},{4,5},{6,7},{8,9},{10,11},{12,13},{14,15},{16,17},{18,... | collective-permute-start | bytes 12296 | tf_op jit(solution)/shard_map/ppermute | solution.py:22
  15.5 5.4 %collective-permute-start.4 = (f32[2,1,64,128]{3,2,1,0:T(8,128)S(1)}, f32[2,1,64,128]{3,2,1,0:T(8,128)S(1)}, u32[]{:S(2)}, u32[]{:S(2)}) collective-permute-start(f32[2,1,64,128]{3,2,1,0:T(8,128)S(1)} %get-tuple-element.23), channel_id=1, source_target_pairs={{2,0},{4,2},{6,4},{8,6},{10,8},{12,10},{14,12},{16,14},{18,16},{20... | collective-permute-start | bytes 196616 | tf_op jit(solution)/shard_map/ppermute | solution.py:24
  16.8 5.0 %collective-permute-start.5 = (f32[2,1,64,128]{3,2,1,0:T(8,128)S(1)}, f32[2,1,64,128]{3,2,1,0:T(8,128)S(1)}, u32[]{:S(2)}, u32[]{:S(2)}) collective-permute-start(f32[2,1,64,128]{3,2,1,0:T(8,128)S(1)} %get-tuple-element.22), channel_id=1, source_target_pairs={{0,2},{2,4},{4,6},{6,8},{8,10},{10,12},{12,14},{14,16},{16,18},{18... | collective-permute-start | bytes 196616 | tf_op jit(solution)/shard_map/ppermute | solution.py:22
  21.8 5.8 %collective-permute-start.6 = (f32[2,4,1,128]{3,2,1,0:T(1,128)S(1)}, f32[2,4,1,128]{3,2,1,0:T(1,128)S(1)}, u32[]{:S(2)}, u32[]{:S(2)}) collective-permute-start(f32[2,4,1,128]{3,2,1,0:T(1,128)S(1)} %get-tuple-element.14), channel_id=1, source_target_pairs={{1,0},{3,2},{5,4},{7,6},{9,8},{11,10},{13,12},{15,14},{17,16},{19,... | collective-permute-start | bytes 12296 | tf_op jit(solution)/shard_map/ppermute | solution.py:24
  23.1 5.9 %collective-permute-start.7 = (f32[2,4,1,128]{3,2,1,0:T(1,128)S(1)}, f32[2,4,1,128]{3,2,1,0:T(1,128)S(1)}, u32[]{:S(2)}, u32[]{:S(2)}) collective-permute-start(f32[2,4,1,128]{3,2,1,0:T(1,128)S(1)} %get-tuple-element.15), channel_id=1, source_target_pairs={{0,1},{2,3},{4,5},{6,7},{8,9},{10,11},{12,13},{14,15},{16,17},{18,... | collective-permute-start | bytes 12296 | tf_op jit(solution)/shard_map/ppermute | solution.py:22
  29.2 7.1 %collective-permute-start.8 = (f32[2,1,64,128]{3,2,1,0:T(8,128)S(1)}, f32[2,1,64,128]{3,2,1,0:T(8,128)S(1)}, u32[]{:S(2)}, u32[]{:S(2)}) collective-permute-start(f32[2,1,64,128]{3,2,1,0:T(8,128)S(1)} %get-tuple-element.21), channel_id=1, source_target_pairs={{2,0},{4,2},{6,4},{8,6},{10,8},{12,10},{14,12},{16,14},{18,16},{20... | collective-permute-start | bytes 196616 | tf_op jit(solution)/shard_map/ppermute | solution.py:24
  30.5 6.7 %collective-permute-start.9 = (f32[2,1,64,128]{3,2,1,0:T(8,128)S(1)}, f32[2,1,64,128]{3,2,1,0:T(8,128)S(1)}, u32[]{:S(2)}, u32[]{:S(2)}) collective-permute-start(f32[2,1,64,128]{3,2,1,0:T(8,128)S(1)} %get-tuple-element.20), channel_id=1, source_target_pairs={{0,2},{2,4},{4,6},{6,8},{8,10},{10,12},{12,14},{14,16},{16,18},{18... | collective-permute-start | bytes 196616 | tf_op jit(solution)/shard_map/ppermute | solution.py:22
  37.2 5.9 %collective-permute-start.10 = (f32[2,4,1,128]{3,2,1,0:T(1,128)S(1)}, f32[2,4,1,128]{3,2,1,0:T(1,128)S(1)}, u32[]{:S(2)}, u32[]{:S(2)}) collective-permute-start(f32[2,4,1,128]{3,2,1,0:T(1,128)S(1)} %get-tuple-element.12), channel_id=1, source_target_pairs={{1,0},{3,2},{5,4},{7,6},{9,8},{11,10},{13,12},{15,14},{17,16},{19,... | collective-permute-start | bytes 12296 | tf_op jit(solution)/shard_map/ppermute | solution.py:24
  38.5 5.9 %collective-permute-start.11 = (f32[2,4,1,128]{3,2,1,0:T(1,128)S(1)}, f32[2,4,1,128]{3,2,1,0:T(1,128)S(1)}, u32[]{:S(2)}, u32[]{:S(2)}) collective-permute-start(f32[2,4,1,128]{3,2,1,0:T(1,128)S(1)} %get-tuple-element.13), channel_id=1, source_target_pairs={{0,1},{2,3},{4,5},{6,7},{8,9},{10,11},{12,13},{14,15},{16,17},{18,... | collective-permute-start | bytes 12296 | tf_op jit(solution)/shard_map/ppermute | solution.py:22
  44.5 7.4 %collective-permute-start.12 = (f32[2,1,64,128]{3,2,1,0:T(8,128)S(1)}, f32[2,1,64,128]{3,2,1,0:T(8,128)S(1)}, u32[]{:S(2)}, u32[]{:S(2)}) collective-permute-start(f32[2,1,64,128]{3,2,1,0:T(8,128)S(1)} %get-tuple-element.19), channel_id=1, source_target_pairs={{2,0},{4,2},{6,4},{8,6},{10,8},{12,10},{14,12},{16,14},{18,16},{20... | collective-permute-start | bytes 196616 | tf_op jit(solution)/shard_map/ppermute | solution.py:24
  45.8 6.9 %collective-permute-start.13 = (f32[2,1,64,128]{3,2,1,0:T(8,128)S(1)}, f32[2,1,64,128]{3,2,1,0:T(8,128)S(1)}, u32[]{:S(2)}, u32[]{:S(2)}) collective-permute-start(f32[2,1,64,128]{3,2,1,0:T(8,128)S(1)} %get-tuple-element.18), channel_id=1, source_target_pairs={{0,2},{2,4},{4,6},{6,8},{8,10},{10,12},{12,14},{14,16},{16,18},{18... | collective-permute-start | bytes 196616 | tf_op jit(solution)/shard_map/ppermute | solution.py:22
  52.7 5.9 %collective-permute-start.14 = (f32[2,4,1,128]{3,2,1,0:T(1,128)S(1)}, f32[2,4,1,128]{3,2,1,0:T(1,128)S(1)}, u32[]{:S(2)}, u32[]{:S(2)}) collective-permute-start(f32[2,4,1,128]{3,2,1,0:T(1,128)S(1)} %get-tuple-element.10), channel_id=1, source_target_pairs={{1,0},{3,2},{5,4},{7,6},{9,8},{11,10},{13,12},{15,14},{17,16},{19,... | collective-permute-start | bytes 12296 | tf_op jit(solution)/shard_map/ppermute | solution.py:24
  54.0 5.9 %collective-permute-start.15 = (f32[2,4,1,128]{3,2,1,0:T(1,128)S(1)}, f32[2,4,1,128]{3,2,1,0:T(1,128)S(1)}, u32[]{:S(2)}, u32[]{:S(2)}) collective-permute-start(f32[2,4,1,128]{3,2,1,0:T(1,128)S(1)} %get-tuple-element.11), channel_id=1, source_target_pairs={{0,1},{2,3},{4,5},{6,7},{8,9},{10,11},{12,13},{14,15},{16,17},{18,... | collective-permute-start | bytes 12296 | tf_op jit(solution)/shard_map/ppermute | solution.py:22
  62.3 7.3 %all-to-all-start = ((f32[2,1,512]{2,1,0:T(1,128)}), f32[2,1,512]{2,1,0:T(1,128)S(1)}, u32[]{:S(2)}, u32[]{:S(2)}) async-start(f32[2,1,512]{2,1,0:T(1,128)} %reshape.169), calls=%async_computation | async-start | bytes 8192 | tf_op jit(solution)/shard_map/all_to_all | solution.py:82
